TPU v7x, 32 devices: a whole 2x2x4 slice. The times are simulated.
32 devices in a mesh: tile: 8 (over z, y), cuts: 4 (over x, core).
Axes of the slice: x: 2, y: 2, z: 4, core: 2. Of those that a mesh axis runs over, the one named last changes fastest.
Arguments:
- object_slices: float32 [8, 2, 2048, 256], P('cuts', None, 'tile'), may hold values from -1 to 1, as said below
- probe_field: float32 [2, 256, 256], replicated, may hold values from -6 to 6
- row_offsets: int32 [32], P('tile'), may hold values from 0 to 255, as said below
- columns: int32 [32], P('tile'), may hold values from 0 to 0
- counts: int32 [8], P('tile'), may hold values from 1 to 4, 16 in all
- amplitudes: bfloat16 [32, 256, 256], P('tile'), may hold values from 0.25 to 4
Outputs:
- new_object: float32 [8, 2, 2048, 256], P('cuts', None, 'tile')
Inputs may be any that keep to these rules, and one draw needn't show every extreme that they name: `row_offsets`: the patch of slot k of block b starts at object row b * 256 + value; in the last block values are at most 0, so every patch lies inside the object and inside its own tile and the next one. `counts`: block b uses its first value slots; the others are padding. The values sum to 16. `object_slices`: every entry has magnitude at most 1.
All inputs are finite; a program needn't handle non-finite values.
Results may differ from a plain program's by a relative error of at most 0.015.
Values may be sent and summed in bfloat16 or wider, within the bound.
A program may use at most 64 MiB of HBM per device.

v0:
```python
import functools
import math

import jax
import jax.numpy as jnp
import numpy as np
from jax import lax
from jax.experimental import pallas as pl
from jax.experimental.pallas import tpu as pltpu
from jax.sharding import PartitionSpec as P

PAT = 256
HALF = PAT // 2
ITERS = 2
RATE = 0.25
BF16 = jnp.bfloat16
F32 = jnp.float32
MESH = pl.DeviceIdType.MESH


def tables(size):
    index = np.arange(size)
    angle = (index[:, None] * index[None, :] % size) * (2.0 * math.pi / size)
    cosine, sine = np.cos(angle), np.sin(angle)
    signed = np.where(index < size // 2, index, index - size)
    phase = (signed * signed % (8 * size)) * (-math.pi / (4.0 * size))
    filter_re, filter_im = np.cos(phase), np.sin(phase)
    kernel_re = (filter_re @ cosine - filter_im @ sine) / size
    kernel_im = (filter_re @ sine + filter_im @ cosine) / size
    offset = (index[:, None] - index[None, :]) % size
    norm = 1.0 / math.sqrt(size)

    def rounded(a):
        return a.astype(np.float32).astype(jnp.bfloat16)

    def four(re, im):
        re, im = rounded(re), rounded(im)
        left = np.concatenate([np.concatenate([re, -im], 1), np.concatenate([im, re], 1)], 0)
        right = np.concatenate([np.concatenate([re, im], 1), np.concatenate([-im, re], 1)], 0)
        rows = np.arange(2 * size).reshape(2, 2, size // 2).swapaxes(0, 1).reshape(-1)
        return np.stack([left[:, rows], right, right[:, rows], left])

    return four(kernel_re[offset], kernel_im[offset]), four(cosine * norm, -sine * norm)


def dot(left, right):
    return jnp.dot(left, right, preferred_element_type=F32)


def beside(mid):
    mid = mid.astype(BF16)
    return jnp.concatenate([mid[:PAT], mid[PAT:]], axis=1)


def halves(full):
    full = full.astype(BF16)
    return [stacked(full[h : h + HALF, :PAT], full[h : h + HALF, PAT:]) for h in (0, HALF)]


def stacked(re, im):
    return jnp.concatenate([re.astype(BF16), im.astype(BF16)], axis=0)


def transform(tabs, which, field):
    mid = dot(tabs[which], jnp.concatenate(field, axis=0))
    return dot(beside(mid), tabs[which + 1])


def shifted(block, shift):
    turned = pltpu.roll(block, (8 - shift) & 7, 1)
    within = lax.broadcasted_iota(jnp.int32, turned[1:].shape, 1) < 8 - shift
    return jnp.where(within, turned[:-1], turned[1:])


def kernel(
    places, counts, obj_in, probe_in, amps_in, prop_in, four_in, out,
    obj, probe, amps, prop, four, ext, grads, padded, win, psi, kept_g, sent_psi, got_g, sent_g, sent_dn, sent_up, got_dn, got_up,
    psi_ss, psi_rs, g_ss, g_rs, dn_ss, dn_rs, up_ss, up_rs,
    in_sems, go,
):
    depth, _, rows, width = obj.shape
    slots = amps.shape[0]
    own, reach, pat = rows // 8, (rows + PAT) // 8, PAT // 8
    cut, cuts = lax.axis_index("cuts"), lax.axis_size("cuts")
    tile, tiles = lax.axis_index("tile"), lax.axis_size("tile")
    not_first, not_last = cut > 0, cut < cuts - 1
    has_before, has_after = tile > 0, tile < tiles - 1

    slice_loads = [
        pltpu.make_async_copy(obj_in.at[l], obj.at[l], in_sems.at[l]) for l in range(depth)
    ]
    loads = [
        pltpu.make_async_copy(src, dst, in_sems.at[depth + i])
        for i, (src, dst) in enumerate(
            ((prop_in, prop), (probe_in, probe), (four_in, four), (amps_in, amps)))
    ]
    for load in slice_loads + loads:
        load.start()

    barrier = pltpu.get_barrier_semaphore()
    for there, where in (
        (not_first, {"cuts": cut - 1}),
        (not_last, {"cuts": cut + 1}),
        (has_before, {"tile": tile - 1}),
        (has_after, {"tile": tile + 1}),
    ):
        @pl.when(there)
        def _(where=where):
            pl.semaphore_signal(barrier, inc=1, device_id=where, device_id_type=MESH)
    neighbours = sum(
        there.astype(jnp.int32) for there in (not_first, not_last, has_before, has_after)
    )
    pl.semaphore_wait(barrier, neighbours)

    def copy_psi(it, slot, h):
        return pltpu.make_async_remote_copy(
            sent_psi.at[it, slot, h], psi.at[it, slot, 0, h],
            psi_ss.at[it, slot, h], psi_rs.at[it, slot, h],
            device_id={"cuts": cut + 1}, device_id_type=MESH)

    def copy_g(it, slot, h):
        return pltpu.make_async_remote_copy(
            sent_g.at[it, slot, h], got_g.at[it, slot, h],
            g_ss.at[it, slot, h], g_rs.at[it, slot, h],
            device_id={"cuts": cut - 1}, device_id_type=MESH)

    def copy_dn(stage, l):
        return pltpu.make_async_remote_copy(
            sent_dn.at[stage, l], got_dn.at[stage, l], dn_ss.at[stage, l], dn_rs.at[stage, l],
            device_id={"tile": tile - 1}, device_id_type=MESH)

    def copy_up(it, l):
        return pltpu.make_async_remote_copy(
            sent_up.at[it, l], got_up.at[it, l], up_ss.at[it, l], up_rs.at[it, l],
            device_id={"tile": tile + 1}, device_id_type=MESH)

    for l in range(depth):
        slice_loads[l].wait()
        sent_dn[0, l] = obj[l, :, :PAT].astype(BF16)
        if l == 0:
            @pl.when(cut == 1)
            def _():
                pl.semaphore_wait(go, 1)

        @pl.when(has_before)
        def _(l=l):
            copy_dn(0, l).start()

    for load in loads:
        load.wait()

    for stage in range(ITERS):
        @pl.when(jnp.logical_not(has_after))
        def _(stage=stage):
            got_dn[stage] = jnp.zeros(got_dn.shape[1:], BF16)

        @pl.when(jnp.logical_not(has_before))
        def _(stage=stage):
            got_up[stage] = jnp.zeros(got_up.shape[1:], BF16)

    @pl.when(jnp.logical_not(not_first))
    def _():
        for h in range(2):
            at = pl.ds(h * HALF, HALF)
            start = stacked(probe[0, at], probe[1, at])
            for it in range(ITERS):
                for slot in range(slots):
                    psi[it, slot, 0, h] = start

        @pl.when(has_before)
        def _():
            for l in range(depth):
                copy_dn(0, l).wait_send()

        if cuts > 1:
            pl.semaphore_signal(go, inc=1, device_id={"cuts": cut + 1}, device_id_type=MESH)

    for part in range(2):
        padded[part, :pat] = jnp.zeros((pat, 8, width), F32)
        padded[part, 2 * pat :] = jnp.zeros((own + 1, 8, width), F32)

    def eights(block):
        return block.reshape(block.shape[:-2] + (block.shape[-2] // 8, 8, width))

    def flat(block):
        return block.reshape(block.shape[:-3] + (block.shape[-3] * 8, width))

    def prepare(it, l):
        @pl.when(has_after)
        def _():
            copy_dn(it, l).wait_recv()

        @pl.when(it == 0)
        def _():
            ext[l, :, :own] = eights(obj[l])
            ext[l, :, own:] = eights(got_dn[0, l].astype(F32))

        @pl.when(it > 0)
        def _():
            @pl.when(has_before)
            def _():
                copy_up(it - 1, l).wait_recv()

            ext[l, :, :own] = updated(it - 1, l)
            ext[l, :, own:] -= RATE * (grads[l, :, own:] + eights(got_dn[it, l].astype(F32)))

    def extract(slot, l):
        place = places[0, slot]
        for part in range(2):
            block = ext[l, part, pl.ds(place, pat + 1)]
            win[slot, l, part] = flat(shifted(block, places[1, slot]))

    def updated(it, l):
        top = ext[l, :, :pat] - RATE * (grads[l, :, :pat] + eights(got_up[it, l].astype(F32)))
        if own == pat:
            return top
        rest = ext[l, :, pat:own] - RATE * grads[l, :, pat:own]
        return jnp.concatenate([top, rest], axis=1)

    def forward(it, slot):
        @pl.when(jnp.logical_and(not_first, slot == 0))
        def _():
            for l in range(depth):
                prepare(it, l)
                for each in range(slots):
                    extract(each, l)

        for l in range(depth):
            @pl.when(jnp.logical_not(not_first))
            def _(l=l):
                @pl.when(slot == 0)
                def _():
                    prepare(it, l)

                extract(slot, l)

            field, mid = [], 0.0
            for h in range(2):
                if l == 0:
                    @pl.when(not_first)
                    def _(h=h):
                        copy_psi(it, slot, h).wait_recv()

                at = pl.ds(h * HALF, HALF)
                w_re, w_im = win[slot, l, 0, at], win[slot, l, 1, at]
                f_re = psi[it, slot, l, h, :HALF].astype(F32)
                f_im = psi[it, slot, l, h, HALF:].astype(F32)
                field.append(stacked(f_re * w_re - f_im * w_im, f_re * w_im + f_im * w_re))
                if l < depth - 1:
                    mid += dot(prop[0, :, h * PAT : (h + 1) * PAT], field[h])

            if l < depth - 1:
                for h, half in enumerate(halves(dot(beside(mid), prop[1]))):
                    psi[it, slot, l + 1, h] = half
                continue

            @pl.when(not_last)
            def _():
                mid = beside(dot(prop[0], jnp.concatenate(field, axis=0)))
                for h in range(2):
                    full = dot(mid[h * HALF : (h + 1) * HALF], prop[1])
                    sent_psi[it, slot, h] = stacked(full[:, :PAT], full[:, PAT:])
                    copy_psi(it, slot, h).start()

            @pl.when(jnp.logical_not(not_last))
            def _():
                far = transform(four, 0, field)
                far_re, far_im = far[:, :PAT], far[:, PAT:]
                mask = jnp.where(slot < counts[0], 1.0, 0.0).astype(F32)
                modulus = jnp.sqrt(far_re * far_re + far_im * far_im + 1.0)
                factor = mask * (1.0 - amps[slot].astype(F32) / modulus)
                chi = halves(jnp.concatenate([far_re * factor, far_im * factor], axis=1))
                for h, half in enumerate(halves(transform(four, 2, chi))):
                    kept_g[slot, l, h] = half

    def backward(it, slot):
        @pl.when(not_last)
        def _():
            mid = 0.0
            for h in range(2):
                copy_g(it, slot, h).wait_recv()
                mid += dot(prop[2, :, h * PAT : (h + 1) * PAT], got_g[it, slot, h])
            for h, half in enumerate(halves(dot(beside(mid), prop[3]))):
                kept_g[slot, depth - 1, h] = half

        def adjoint(l, h):
            at = pl.ds(h * HALF, HALF)
            w_re, w_im = win[slot, l, 0, at], win[slot, l, 1, at]
            g_re = kept_g[slot, l, h, :HALF].astype(F32)
            g_im = kept_g[slot, l, h, HALF:].astype(F32)
            return stacked(w_re * g_re + w_im * g_im, w_re * g_im - w_im * g_re)

        for l in reversed(range(1, depth)):
            full = transform(prop, 2, [adjoint(l, 0), adjoint(l, 1)])
            for h, half in enumerate(halves(full)):
                kept_g[slot, l - 1, h] = half

        @pl.when(not_first)
        def _():
            for h in range(2):
                sent_g[it, slot, h] = adjoint(0, h)
                copy_g(it, slot, h).start()

    def accumulate(it, slot):
        for l in range(depth):
            for h in range(2):
                g_re = kept_g[slot, l, h, :HALF].astype(F32)
                g_im = kept_g[slot, l, h, HALF:].astype(F32)
                f_re = psi[it, slot, l, h, :HALF].astype(F32)
                f_im = psi[it, slot, l, h, HALF:].astype(F32)
                at = pl.ds(pat + h * (pat // 2), pat // 2)
                padded[0, at] = eights(f_re * g_re + f_im * g_im)
                padded[1, at] = eights(f_re * g_im - f_im * g_re)
            place = places[2, slot]
            for part in range(2):
                block = padded[part, pl.ds(place, reach + 1)]
                before = jnp.where(slot == 0, 0.0, grads[l, part])
                grads[l, part] = before + shifted(block, places[3, slot])

            @pl.when(slot == slots - 1)
            def _(l=l):
                @pl.when(has_after)
                def _():
                    sent_up[it, l] = flat(grads[l, :, own:]).astype(BF16)
                    copy_up(it, l).start()

                @pl.when(jnp.logical_and(has_before, it < ITERS - 1))
                def _():
                    sent_dn[it + 1, l] = flat(grads[l, :, :pat]).astype(BF16)
                    copy_dn(it + 1, l).start()

    lag = jnp.minimum(cuts - 1 - cut, 2)
    lag = jnp.where(lag == 2, slots - 1, lag)

    def step(index, _):
        it, at = index // (2 * slots - 1), index % (2 * slots - 1)

        @pl.when(at < slots)
        def _():
            forward(it, at)

        @pl.when(jnp.logical_and(at >= lag, at < lag + slots))
        def _():
            backward(it, at - lag)

        @pl.when(at >= slots - 1)
        def _():
            accumulate(it, at - (slots - 1))

        return 0

    lax.fori_loop(0, ITERS * (2 * slots - 1), step, 0)

    for l in reversed(range(depth)):
        @pl.when(has_before)
        def _(l=l):
            copy_up(ITERS - 1, l).wait_recv()

        out[l] = flat(updated(ITERS - 1, l))

    for it in range(ITERS):
        for slot in range(slots):
            @pl.when(not_last)
            def _(it=it, slot=slot):
                for h in range(2):
                    copy_psi(it, slot, h).wait_send()

            @pl.when(not_first)
            def _(it=it, slot=slot):
                for h in range(2):
                    copy_g(it, slot, h).wait_send()

        for l in range(depth):
            @pl.when(has_after)
            def _(it=it, l=l):
                copy_up(it, l).wait_send()

            @pl.when(jnp.logical_and(has_before, jnp.logical_or(not_first, it > 0)))
            def _(it=it, l=l):
                copy_dn(it, l).wait_send()


def local(object_slices, probe_field, row_offsets, columns, counts, amplitudes):
    depth, _, rows, width = object_slices.shape
    slots = amplitudes.shape[0]
    prop, four = tables(PAT)
    back = PAT - row_offsets
    places = jnp.stack([row_offsets // 8, row_offsets % 8, back // 8, back % 8])
    dma = pltpu.SemaphoreType.DMA
    vmem, smem = pltpu.VMEM, pltpu.SMEM
    return pl.pallas_call(
        kernel,
        out_shape=jax.ShapeDtypeStruct(object_slices.shape, F32),
        in_specs=[pl.BlockSpec(memory_space=smem)] * 2 + [pl.BlockSpec(memory_space=pl.ANY)] * 5,
        out_specs=pl.BlockSpec(memory_space=vmem),
        scratch_shapes=[
            vmem(object_slices.shape, F32),
            vmem(probe_field.shape, F32),
            vmem(amplitudes.shape, BF16),
            vmem(prop.shape, BF16),
            vmem(four.shape, BF16),
            vmem((depth, 2, (rows + PAT) // 8, 8, width), F32),
            vmem((depth, 2, (rows + PAT) // 8, 8, width), F32),
            vmem((2, (2 * PAT + rows) // 8 + 1, 8, width), F32),
            vmem((slots, depth, 2, PAT, width), F32),
            vmem((ITERS, slots, depth, 2, PAT, PAT), BF16),
            vmem((slots, depth, 2, PAT, PAT), BF16),
            vmem((ITERS, slots, 2, PAT, PAT), BF16),
            vmem((ITERS, slots, 2, PAT, PAT), BF16),
            vmem((ITERS, slots, 2, PAT, PAT), BF16),
            vmem((ITERS, depth, 2, PAT, width), BF16),
            vmem((ITERS, depth, 2, PAT, width), BF16),
            vmem((ITERS, depth, 2, PAT, width), BF16),
            vmem((ITERS, depth, 2, PAT, width), BF16),
            dma((ITERS, slots, 2)), dma((ITERS, slots, 2)),
            dma((ITERS, slots, 2)), dma((ITERS, slots, 2)),
            dma((ITERS, depth)), dma((ITERS, depth)),
            dma((ITERS, depth)), dma((ITERS, depth)),
            dma((depth + 4,)), pltpu.SemaphoreType.REGULAR,
        ],
        compiler_params=pltpu.CompilerParams(
            collective_id=0, has_side_effects=True, vmem_limit_bytes=58 * 1024 * 1024),
    )(places, counts, object_slices, probe_field, amplitudes, jnp.asarray(prop), jnp.asarray(four))


def solution(mesh):
    in_specs = (
        P("cuts", None, "tile", None),
        P(),
        P("tile"),
        P("tile"),
        P("tile"),
        P("tile", None, None),
    )
    out_specs = P("cuts", None, "tile", None)
    return jax.shard_map(local, mesh=mesh, in_specs=in_specs, out_specs=out_specs, check_vma=False)
```

profile of v0, /device:TPU:8, one launch (start us, length us, event | category | flops | bytes accessed | tf_op | source)
XLA Modules:
  0.0 130.9 jit_solution(8289738011993483303)
XLA Ops:
  0.7 0.7 fusion.3
  1.3 0.6 pad_add_fusion.places
  1.9 126.7 %shard_map.73 = f32[2,2,256,256]{3,2,1,0:T(8,128)} custom-call(s32[4,4]{1,0:T(4,128)} %pad_add_fusion.places, s32[1]{0:T(128)S(6)} %copy.9.counts, f32[2,2,256,256]{3,2,1,0:T(8,128)} %obj_in.1, f32[2,256,256]{2,1,0:T(8,128)} %probe_in.1, bf16[4,256,256]{2,1,0:T(8,128)(2,1)} %amps_in.1, bf16[4,512,512]{2,1,0:T(8,128)(2,1)} %constant.46.clone.prop_in, ...), custom_call_target="tpu_custom_call" | custom-call | tf_op jit(solution)/shard_map/pallas_call | solution.py:391
  128.6 2.3 %copy.10 = f32[2,2,256,256]{3,2,1,0:T(8,128)} copy(f32[2,2,256,256]{3,2,1,0:T(8,128)} %shard_map.73) | data formatting | bytes 2097152
  (1 shorter events, 0.0 us)
where the time goes:
time: 131 us
  Pallas kernels  127 us (97%)
  local copies, waits for them, and re-layouts  2.29 us (2%)
    pallas_call x1, Pallas kernels, local(): pl.pallas_call(kernel, out_shape=jax.ShapeDtypeStruct(object_slices.shape...  127 us

commit v1 on v0

--- a/solution.py
+++ b/solution.py
@@ -62,8 +62,10 @@
 
 
 def transform(tabs, which, field):
-    mid = dot(tabs[which], jnp.concatenate(field, axis=0))
-    return dot(beside(mid), tabs[which + 1])
+    field = jnp.concatenate(field, axis=0)
+    mid_re = dot(tabs[which, :PAT], field).astype(BF16)
+    mid_im = dot(tabs[which, PAT:], field).astype(BF16)
+    return dot(mid_re, tabs[which + 1, :PAT]) + dot(mid_im, tabs[which + 1, PAT:])
 
 
 def shifted(block, shift):
@@ -234,7 +236,7 @@
 
                 extract(slot, l)
 
-            field, mid = [], 0.0
+            field, mid = [], None
             for h in range(2):
                 if l == 0:
                     @pl.when(not_first)
@@ -247,7 +249,8 @@
                 f_im = psi[it, slot, l, h, HALF:].astype(F32)
                 field.append(stacked(f_re * w_re - f_im * w_im, f_re * w_im + f_im * w_re))
                 if l < depth - 1:
-                    mid += dot(prop[0, :, h * PAT : (h + 1) * PAT], field[h])
+                    term = dot(prop[0, :, h * PAT : (h + 1) * PAT], field[h])
+                    mid = term if mid is None else mid + term
 
             if l < depth - 1:
                 for h, half in enumerate(halves(dot(beside(mid), prop[1]))):
@@ -276,10 +279,11 @@
     def backward(it, slot):
         @pl.when(not_last)
         def _():
-            mid = 0.0
+            mid = None
             for h in range(2):
                 copy_g(it, slot, h).wait_recv()
-                mid += dot(prop[2, :, h * PAT : (h + 1) * PAT], got_g[it, slot, h])
+                term = dot(prop[2, :, h * PAT : (h + 1) * PAT], got_g[it, slot, h])
+                mid = term if mid is None else mid + term
             for h, half in enumerate(halves(dot(beside(mid), prop[3]))):
                 kept_g[slot, depth - 1, h] = half
 

time: 131 us -> 128 us (0.977)
  Pallas kernels: 127 us -> 124 us
    pallas_call x1, Pallas kernels: 127 us -> 124 us  [local(): pl.pallas_call(kernel, out_shape=jax.ShapeDtypeStruct(object_slices.shape...]
where the time goes in v1:
time: 128 us
  Pallas kernels  124 us (97%)
  local copies, waits for them, and re-layouts  2.29 us (2%)
    pallas_call x1, Pallas kernels, local(): pl.pallas_call(kernel, out_shape=jax.ShapeDtypeStruct(object_slices.shape...  124 us

profile of v1, /device:TPU:8, one launch (start us, length us, event | category | flops | bytes accessed | tf_op | source)
XLA Modules:
  0.0 127.7 jit_solution(1290992997419681571)
XLA Ops:
  0.7 0.7 fusion.3
  1.3 0.6 pad_add_fusion.places
  1.9 123.5 %shard_map.73 = f32[2,2,256,256]{3,2,1,0:T(8,128)} custom-call(s32[4,4]{1,0:T(4,128)} %pad_add_fusion.places, s32[1]{0:T(128)S(6)} %copy.9.counts, f32[2,2,256,256]{3,2,1,0:T(8,128)} %obj_in.1, f32[2,256,256]{2,1,0:T(8,128)} %probe_in.1, bf16[4,256,256]{2,1,0:T(8,128)(2,1)} %amps_in.1, bf16[4,512,512]{2,1,0:T(8,128)(2,1)} %constant.46.clone.prop_in, ...), custom_call_target="tpu_custom_call" | custom-call | tf_op jit(solution)/shard_map/pallas_call | solution.py:395
  125.5 2.3 %copy.10 = f32[2,2,256,256]{3,2,1,0:T(8,128)} copy(f32[2,2,256,256]{3,2,1,0:T(8,128)} %shard_map.73) | data formatting | bytes 2097152
  (1 shorter events, 0.0 us)
